TPU v7x, 32 devices: a whole 2x2x4 slice. The times are simulated.
32 devices in a mesh: wa: 8 (over y, x, core), ha: 4 (over z).
Axes of the slice: x: 2, y: 2, z: 4, core: 2. Of those that a mesh axis runs over, the one named last changes fastest.
Arguments:
- residual_in: bfloat16 [48, 16384], P('ha', 'wa'), may hold values from -43.25 to 43.25
- grad_out: bfloat16 [48, 16384], P('ha', 'wa'), may hold values from -6 to 6
- norm_gain: bfloat16 [16384], P('wa'), may hold values from 0.099609375 to 1.8984375
- w_gate: bfloat16 [16384, 26624], P('wa', 'ha'), may hold values from -0.0390625 to 0.0390625
- w_up: bfloat16 [16384, 26624], P('wa', 'ha'), may hold values from -0.0390625 to 0.0390625
- w_down: bfloat16 [26624, 16384], P('ha', 'wa'), may hold values from -0.030643146 to 0.030643146
Outputs:
- grad_in: bfloat16 [48, 16384], P('ha', 'wa')
All inputs are finite; a program needn't handle non-finite values.
Results may differ from a plain program's by a relative error of at most 0.0053.
Values may be sent and summed in bfloat16 or wider, within the bound.
A program may use at most 128 MiB of HBM per device.

v0:
```python
import jax
import jax.numpy as jnp
from jax import lax
from jax.sharding import PartitionSpec as P

D = 16384


def gate_grads(gate, up, d_hidden):
    sig = jax.nn.sigmoid(gate)
    d_up = (d_hidden * gate * sig).astype(jnp.bfloat16)
    d_gate = (d_hidden * up * sig * (1.0 + gate * (1.0 - sig))).astype(jnp.bfloat16)
    return jnp.stack([d_gate, d_up])


def local(residual_in, grad_out, norm_gain, w_gate, w_up, w_down):
    stream = residual_in.astype(jnp.float32)
    squares = lax.psum(jnp.sum(stream * stream, axis=1), "wa")
    inv_rms = lax.rsqrt(squares / D + 1e-05)[:, None]
    gain_f = norm_gain.astype(jnp.float32)
    normed = (stream * inv_rms * gain_f).astype(jnp.bfloat16)
    stacked = jnp.stack([normed, grad_out])
    piece = lax.all_gather(stacked, "ha", axis=1, tiled=True)
    gate_part = jnp.dot(piece[0], w_gate, preferred_element_type=jnp.float32)
    up_part = jnp.dot(piece[0], w_up, preferred_element_type=jnp.float32)
    back_part = lax.dot_general(
        piece[1], w_down, (((1,), (1,)), ((), ())), preferred_element_type=jnp.float32
    )
    partial_sums = jnp.stack([gate_part, up_part, back_part])
    summed = lax.psum(partial_sums, "wa")
    grads = gate_grads(summed[0], summed[1], summed[2])
    total = lax.dot_general(
        grads[0], w_gate, (((1,), (1,)), ((), ())), preferred_element_type=jnp.float32
    )
    d_normed = lax.psum_scatter(
        total
        + lax.dot_general(
            grads[1], w_up, (((1,), (1,)), ((), ())), preferred_element_type=jnp.float32
        ),
        "ha",
        scatter_dimension=0,
        tiled=True,
    )
    scaled = d_normed * gain_f
    row_dot = lax.psum(jnp.sum(scaled * stream, axis=1), "wa")[:, None]
    grad_in = grad_out.astype(jnp.float32) + inv_rms * scaled - stream * inv_rms**3 * row_dot / D
    return grad_in.astype(jnp.bfloat16)


def solution(mesh):
    placed = (P("ha", "wa"), P("ha", "wa"), P("wa"), P("wa", "ha"), P("wa", "ha"), P("ha", "wa"))
    return jax.shard_map(
        local, mesh=mesh, in_specs=placed, out_specs=P("ha", "wa"), check_vma=False
    )
```

profile of v0, /device:TPU:0, one launch (start us, length us, event | category | flops | bytes accessed | tf_op | source)
XLA Modules:
  0.0 228.2 jit_solution(7728154376662795049)
XLA Ops:
  6.5 1.0 fusion.9
  7.5 0.7 convert_element_type.23
  8.2 15.1 %psum.21 = f32[12]{0:T(128)S(1)} all-reduce(f32[12]{0:T(128)S(1)} %fusion.9), channel_id=1, replica_groups=mesh['wa'=8,'ha'=4] {'wa'}, use_global_device_ids=true, to_apply=%region_1.0 | all-reduce | flops 12 | bytes 96 | tf_op jit(solution)/shard_map/psum | solution.py:18
  23.3 0.9 fusion.17
  24.2 0.9 pad_maximum_fusion.1
  25.1 0.1 copy.7
  25.2 15.1 %all_gather.3 = bf16[2,48,2048]{2,0,1:T(2,128)(2,1)S(1)} all-gather(bf16[2,12,2048]{2,0,1:T(2,128)(2,1)S(1)} %copy.7), channel_id=1, replica_groups=mesh['wa'=8,'ha'=4] {'ha'}, dimensions={1}, use_global_device_ids=true | all-gather | bytes 491520 | tf_op jit(solution)/shard_map/all_gather | solution.py:23
  40.3 0.5 fusion.20
  40.9 11.3 %convolution_bitcast_fusion.1 = f32[1,48,6656]{2,1,0:T(8,128)S(1)} fusion(bf16[2048,6656]{1,0:T(8,128)(2,1)} %param.10, bf16[1,48,2048]{2,0,1:T(2,128)(2,1)S(1)} %get-tuple-element.5), kind=kOutput, calls=%fused_computation.1 | convolution fusion | flops 1308622848 | bytes 28737536 | tf_op jit(solution)/shard_map/dot_general | solution.py:25
  52.2 11.3 %convolution_bitcast_fusion.2 = f32[1,48,6656]{2,1,0:T(8,128)S(1)} fusion(bf16[2048,6656]{1,0:T(8,128)(2,1)} %param.9, bf16[1,48,2048]{2,0,1:T(2,128)(2,1)S(1)} %get-tuple-element.5), kind=kOutput, calls=%fused_computation.2 | convolution fusion | flops 1308622848 | bytes 28737536 | tf_op jit(solution)/shard_map/dot_general | solution.py:24
  63.5 14.4 %convolution_bitcast_fusion = f32[1,48,6656]{2,1,0:T(8,128)} fusion(bf16[6656,2048]{1,0:T(8,128)(2,1)} %param.11, bf16[1,48,2048]{2,0,1:T(2,128)(2,1)S(1)} %get-tuple-element.6), kind=kOutput, calls=%fused_computation | convolution fusion | flops 1308622848 | bytes 28737536 | tf_op jit(solution)/shard_map/dot_general | solution.py:26
  77.9 3.4 %pad_maximum_fusion = f32[3,48,6656]{2,1,0:T(8,128)} fusion(f32[1,48,6656]{2,1,0:T(8,128)} %convolution_bitcast_fusion, f32[1,48,6656]{2,1,0:T(8,128)S(1)} %convolution_bitcast_fusion.1, f32[1,48,6656]{2,1,0:T(8,128)S(1)} %convolution_bitcast_fusion.2), kind=kLoop, calls=%fused_computation.3 | loop fusion | flops 1916928 | bytes 7667712 | tf_op jit(solution)/shard_map/stack | solution.py:29
  81.3 0.0 all-reduce.4.cloned.1.call-update
  81.3 76.4 %all-reduce.4.cloned.1.call-done = f32[3,48,6656]{2,1,0:T(8,128)} async-done(((f32[3,48,6656]{2,1,0:T(8,128)}), f32[3,48,6656]{2,1,0:T(8,128)}) %all-reduce.4.cloned.1.call-update) | async-done | bytes 3833872 | tf_op jit(solution)/shard_map/psum | solution.py:30
  157.8 14.0 %fusion.5 = f32[48,2048]{1,0:T(8,128)S(1)} fusion(bf16[2048,6656]{1,0:T(8,128)(2,1)} %param.9, f32[3,48,6656]{2,1,0:T(8,128)} %all-reduce.4.cloned.1.call-done), kind=kOutput, calls=%fused_computation.14 | convolution fusion | flops 1311817728 | bytes 31490048 | tf_op jit(solution)/shard_map/dot_general | solution.py:32
  171.8 13.7 %convolution_add_fusion = f32[48,2048]{1,0:T(8,128)S(1)} fusion(f32[48,2048]{1,0:T(8,128)S(1)} %fusion.5, bf16[2048,6656]{1,0:T(8,128)(2,1)} %param.10, f32[3,48,6656]{2,1,0:T(8,128)} %all-reduce.4.cloned.1.call-done), kind=kOutput, calls=%fused_computation.4 | convolution fusion | flops 1310638080 | bytes 30605312 | tf_op jit(solution)/shard_map/dot_general | solution.py:37
  185.6 18.6 %fusion = f32[16,2048]{1,0:T(8,128)S(1)} fusion(f32[48,2048]{1,0:T(8,128)S(1)} %convolution_add_fusion), kind=kCustom, calls=%all-reduce-scatter | all-reduce-scatter fusion | flops 131073 | bytes 524800
  204.1 1.8 collective-permute-start
  205.9 0.6 dynamic-slice.4
  207.2 1.2 collective-permute-done
  208.4 0.2 concatenate
  208.6 0.1 fusion.16
  208.8 11.8 %psum.23 = f32[12]{0:T(128)S(1)} all-reduce(f32[12]{0:T(128)S(1)} %fusion.16), channel_id=1, replica_groups=mesh['wa'=8,'ha'=4] {'wa'}, use_global_device_ids=true, to_apply=%region_5.0 | all-reduce | flops 12 | bytes 96 | tf_op jit(solution)/shard_map/psum | solution.py:45
  220.6 0.7 fusion.15
  (9 shorter events, 0.0 us)
Async XLA Ops:
  6.5 151.2 %all-reduce.4.cloned.1.call-start = ((), (), s32[]{:S(2)}) async-start(), calls=%async_computation | async-start | bytes 7667712 | tf_op jit(solution)/shard_map/psum | solution.py:30
  171.8 34.1 %copy-start.2 = (u32[32]{0:T(128)S(1)}, u32[32]{0:T(128)}, u32[]{:S(2)}) copy-start(u32[32]{0:T(128)} %constant.13) | copy-start | bytes 388
  185.5 23.1 %copy-start = (bf16[12,2048]{1,0:T(8,128)(2,1)S(1)}, bf16[12,2048]{1,0:T(8,128)(2,1)}, u32[]{:S(2)}) copy-start(bf16[12,2048]{1,0:T(8,128)(2,1)} %param.6) | copy-start | bytes 147460
  185.5 35.1 %copy-start.1 = (bf16[12,2048]{1,0:T(8,128)(2,1)S(1)}, bf16[12,2048]{1,0:T(8,128)(2,1)}, u32[]{:S(2)}) copy-start(bf16[12,2048]{1,0:T(8,128)(2,1)} %param.7) | copy-start | bytes 147460
  204.1 4.3 %collective-permute-start = (f32[12,2048]{1,0:T(8,128)S(1)}, f32[12,2048]{1,0:T(8,128)S(1)}, u32[]{:S(2)}, u32[]{:S(2)}) collective-permute-start(f32[12,2048]{1,0:T(8,128)S(1)} %slice.26), channel_id=1, source_target_pairs={{0,1},{1,2},{2,3},{4,5},{5,6},{6,7},{8,9},{9,10},{10,11},{12,13},{... | collective-permute-start | bytes 294920
Sparse Core Ops, SparseCore 0:
  81.4 76.2 all-reduce.3
where the time goes:
time: 229 us; the launch traced here: 228 us
  waiting for transfers between devices  77.7 us (34%)
  matrix products  64.8 us (28%)
  blocking collectives  60.6 us (26%)
  between operations  14.2 us (6%)
  other arithmetic  7.73 us (3%)
    psum x1, waiting for transfers between devices, local(): summed = lax.psum(partial_sums, 'wa')  76.4 us
    unnamed x1, blocking collectives  18.6 us
    all_gather x1, blocking collectives, local(): piece = lax.all_gather(stacked, 'ha', axis=1, tiled=True)  15.1 us
    psum x1, blocking collectives, local(): squares = lax.psum(jnp.sum(stream * stream, axis=1), 'wa')  15.1 us
    dot_general x1, matrix products, local(): lax.dot_general(piece[1], w_down, (((1,), (1,)), ((), ())), preferred_ele...  14.4 us
    dot_general x1, matrix products, local(): lax.dot_general(grads[0], w_gate, (((1,), (1,)), ((), ())), preferred_ele...  14 us
    dot_general x1, matrix products, local(): lax.dot_general(grads[1], w_up, (((1,), (1,)), ((), ())), preferred_eleme...  13.7 us
    psum x1, blocking collectives, local(): row_dot = lax.psum(jnp.sum(scaled * stream, axis=1), 'wa')[:, None]  11.8 us
  transfers between devices with their start and end apart: 2, of which 2 were waited for; matrix products, arithmetic and copies ran while one was open for 0% of the time, Pallas kernels for 0%

commit v1 on v0

--- a/solution.py
+++ b/solution.py
@@ -1,9 +1,326 @@
+import functools
+
 import jax
 import jax.numpy as jnp
 from jax import lax
+from jax.experimental import pallas as pl
+from jax.experimental.pallas import tpu as pltpu
 from jax.sharding import PartitionSpec as P
 
+MESH = pl.DeviceIdType.MESH
 D = 16384
+CHUNKS = 13
+SLOTS = 4
+DEEP = 8
+DEEP_DOWN = 6
+F32, BF16 = jnp.float32, jnp.bfloat16
+NT = (((1,), (1,)), ((), ()))
+
+
+def fused(n_wa, n_ha, res, go, gain, wg, wu, wd, out,
+          wgs, wus, wds, xb, tmp, xf, gf, xs, gos, sq, sq_in, inv_half, inv_own,
+          part, pair_in, rs_out, rs_in, gb, acc, rd, rd_in, rz, rz_in, own, fs, fr, tail,
+          g_sem, u_sem, d_sem, x_ss, x_rs, sq_ss, sq_rs, p_ss, p_rs, r_ss, r_rs,
+          a_ss, a_rs, f_ss, f_rs, rd_ss, rd_rs, rz_ss, rz_rs, t_ss, t_rs):
+    me, z = lax.axis_index("wa"), lax.axis_index("ha")
+    chip, core = me // 2, me % 2
+    n_chip = n_wa // 2
+    r, width = res.shape
+    rows, half, wide, cols4 = r * n_ha, r * n_ha // 2, width // 2, width // 4
+    ch = wg.shape[1] // CHUNKS
+    sub = ch // n_chip
+
+    def columns(c):
+        return pl.ds(pl.multiple_of(c * ch, ch), ch)
+
+    def load_g(c):
+        return pltpu.make_async_copy(wg.at[:, columns(c)], wgs.at[c % DEEP], g_sem.at[c % DEEP])
+
+    def load_u(c):
+        return pltpu.make_async_copy(wu.at[:, columns(c)], wus.at[c % DEEP], u_sem.at[c % DEEP])
+
+    def load_d(c):
+        return pltpu.make_async_copy(wd.at[columns(c), :], wds.at[c % DEEP_DOWN], d_sem.at[c % DEEP_DOWN])
+
+    def remote(src, dst, ss, rs, wa, ha):
+        return pltpu.make_async_remote_copy(
+            src_ref=src, dst_ref=dst, send_sem=ss, recv_sem=rs,
+            device_id=(wa, ha), device_id_type=MESH)
+
+    def peer_chip(d):
+        return (chip ^ d) * 2 + core
+
+    for c in range(min(DEEP, CHUNKS)):
+        load_g(c).start()
+        load_u(c).start()
+        if c < DEEP_DOWN:
+            load_d(c).start()
+
+    barrier = pltpu.get_barrier_semaphore()
+    for d in range(1, n_ha):
+        pl.semaphore_signal(barrier, inc=1, device_id=(me, z ^ d), device_id_type=MESH)
+    for d in range(1, n_wa):
+        pl.semaphore_signal(barrier, inc=1, device_id=(me ^ d, z), device_id_type=MESH)
+
+    for j, ref in enumerate((res, go)):
+        for h in range(2):
+            at = (2 * j + h) * r
+            tmp[at:at + r, :] = ref[:, h * wide:(h + 1) * wide].astype(F32)
+    xb[z] = tmp[...].astype(BF16)
+    pl.semaphore_wait(barrier, n_ha + n_wa - 2)
+
+    def gather(d):
+        return remote(xb.at[z], xb.at[z], x_ss.at[d - 1], x_rs.at[d - 1], me, z ^ d)
+
+    for d in range(1, n_ha):
+        gather(d).start()
+    acc[...] = jnp.zeros_like(acc)
+    rd[...] = jnp.zeros_like(rd)
+    rz[...] = jnp.zeros_like(rz)
+    for d in range(1, n_ha):
+        gather(d).wait()
+    for k in range(n_ha):
+        tmp[...] = xb[k].astype(F32)
+        for j, ref in enumerate((xf, gf)):
+            for h in range(2):
+                at = (2 * j + h) * r
+                ref[k * r:(k + 1) * r, h * wide:(h + 1) * wide] = tmp[at:at + r, :]
+    x = xf[...]
+    xs[...] = (x * gain[...]).astype(BF16)
+    gos[...] = gf[...].astype(BF16)
+    lanes = x[:, 0:128] * x[:, 0:128]
+    for j in range(1, width // 128):
+        piece = x[:, j * 128:(j + 1) * 128]
+        lanes = lanes + piece * piece
+    sq[...] = lanes
+
+    def squares(d):
+        return remote(sq, sq_in.at[d - 1], sq_ss.at[d - 1], sq_rs.at[d - 1], me ^ d, z)
+
+    for d in range(1, n_wa):
+        squares(d).start()
+
+    def pair(c):
+        s = c % SLOTS
+        return remote(part.at[s, 1 - core], pair_in.at[s], p_ss.at[s], p_rs.at[s], me ^ 1, z)
+
+    def scatter(c, d):
+        s = c % SLOTS
+        return remote(rs_out.at[s, chip ^ d], rs_in.at[s, d - 1], r_ss.at[s, d - 1], r_rs.at[s, d - 1],
+                      peer_chip(d), z)
+
+    def spread(c, d):
+        s = c % SLOTS
+        return remote(gb.at[c, core, chip], gb.at[c, core, chip], a_ss.at[s, d - 1], a_rs.at[s, d - 1],
+                      peer_chip(d), z)
+
+    def forward(c):
+        s = c % SLOTS
+        return remote(gb.at[c, core], gb.at[c, core], f_ss.at[s], f_rs.at[s], me ^ 1, z)
+
+    def share_rd(d):
+        return remote(rd, rd_in.at[d - 1], rd_ss.at[d - 1], rd_rs.at[d - 1], me ^ d, z)
+
+    def step(i, carry):
+        @pl.when(i < CHUNKS)
+        def _():
+            s = i % SLOTS
+            load_g(i).wait()
+            load_u(i).wait()
+            load_d(i).wait()
+            a = xs[...]
+            gate = jnp.dot(a, wgs[i % DEEP], preferred_element_type=F32)
+            up = jnp.dot(a, wus[i % DEEP], preferred_element_type=F32)
+            back = lax.dot_general(gos[...], wds[i % DEEP_DOWN], NT, preferred_element_type=F32)
+            for h in range(2):
+                for j, v in enumerate((gate, up, back)):
+                    part[s, h, j * half:(j + 1) * half, :] = v[h * half:(h + 1) * half, :]
+            pair(i).start()
+
+            @pl.when(i + DEEP_DOWN < CHUNKS)
+            def _():
+                load_d(i + DEEP_DOWN).start()
+
+        @pl.when((i >= 1) & (i < CHUNKS + 1))
+        def _():
+            c = i - 1
+            s = c % SLOTS
+            pair(c).wait()
+            both = part[s, core] + pair_in[s]
+            for k in range(n_chip):
+                rs_out[s, k] = both[:, k * sub:(k + 1) * sub]
+            for d in range(1, n_chip):
+                scatter(c, d).start()
+
+        @pl.when(i == 2)
+        def _():
+            for d in range(1, n_wa):
+                squares(d).wait()
+            total = sq[...]
+            for d in range(1, n_wa):
+                total = total + sq_in[d - 1]
+            inv = lax.rsqrt(jnp.sum(total, axis=1, keepdims=True) / D + 1e-05)
+            wide_inv = jnp.broadcast_to(inv, (rows, 128))
+            for h in range(2):
+                inv_half[h] = wide_inv[h * half:(h + 1) * half, :]
+            xf[:, 0:128] = wide_inv
+            for k in range(n_ha):
+                inv_own[k] = xf[k * r:(k + 1) * r, 0:128]
+
+        @pl.when((i >= 2) & (i < CHUNKS + 2))
+        def _():
+            c = i - 2
+            s = c % SLOTS
+            for d in range(1, n_chip):
+                scatter(c, d).wait()
+            total = rs_out[s, chip]
+            for d in range(1, n_chip):
+                total = total + rs_in[s, d - 1]
+            inv = inv_half[core][:, 0:1]
+            gate, up, d_hidden = total[:half] * inv, total[half:2 * half] * inv, total[2 * half:]
+            sig = jax.nn.sigmoid(gate)
+            d_up = d_hidden * gate * sig
+            d_gate = d_hidden * up * sig * (1.0 + gate * (1.0 - sig))
+            stacked = jnp.concatenate([d_gate, d_up], axis=0).astype(BF16)
+            gb[c, core, chip] = stacked
+            for d in range(1, n_chip):
+                spread(c, d).start()
+            kept = stacked.astype(F32)
+            terms = kept[:half] * gate + kept[half:] * up
+            for j in range(sub // 128):
+                rd[...] += terms[:, j * 128:(j + 1) * 128]
+
+        @pl.when(i == CHUNKS + 1)
+        def _():
+            for d in range(1, n_wa):
+                share_rd(d).start()
+
+        @pl.when((i >= 3) & (i < CHUNKS + 3))
+        def _():
+            c = i - 3
+            for d in range(1, n_chip):
+                spread(c, d).wait()
+            forward(c).start()
+
+        @pl.when(i >= 4)
+        def _():
+            c = i - 4
+            s = c % DEEP
+            forward(c).wait()
+            halves = [
+                jnp.concatenate([gb[c, h, k] for k in range(n_chip)], axis=1).astype(F32)
+                for h in range(2)
+            ]
+            d_gate = jnp.concatenate([v[:half] for v in halves], axis=0).astype(BF16)
+            d_up = jnp.concatenate([v[half:] for v in halves], axis=0).astype(BF16)
+            for j in range(4):
+                at = slice(j * cols4, (j + 1) * cols4)
+                acc[:, at] += lax.dot_general(
+                    d_gate, wgs[s, at, :], NT, preferred_element_type=F32
+                ) + lax.dot_general(d_up, wus[s, at, :], NT, preferred_element_type=F32)
+
+            @pl.when(c + DEEP < CHUNKS)
+            def _():
+                load_g(c + DEEP).start()
+                load_u(c + DEEP).start()
+
+        return carry
+
+    lax.fori_loop(0, CHUNKS + 4, step, 0)
+
+    for k in range(n_ha):
+        own[k] = acc[k * r:(k + 1) * r, :]
+        for q in range(4):
+            tail[q * r:(q + 1) * r, :] = acc[k * r:(k + 1) * r, q * cols4:(q + 1) * cols4]
+        fs[k] = tail[...].astype(BF16)
+
+    def finish(d):
+        return remote(fs.at[z ^ d], fr.at[d - 1], t_ss.at[d - 1], t_rs.at[d - 1], me, z ^ d)
+
+    for d in range(1, n_ha):
+        finish(d).start()
+
+    for d in range(1, n_wa):
+        share_rd(d).wait()
+    same, other = rd[...], rd_in[0]
+    for d in range(2, n_wa, 2):
+        same, other = same + rd_in[d - 1], other + rd_in[d]
+    low = jnp.where(core == 0, same, other)
+    high = jnp.where(core == 0, other, same)
+    xf[0:half, 0:128] = low
+    xf[half:rows, 0:128] = high
+    for k in range(n_ha):
+        rz[k, 0:r, :] = xf[k * r:(k + 1) * r, 0:128]
+
+    def share_rz(d):
+        return remote(rz.at[z ^ d], rz_in.at[d - 1], rz_ss.at[d - 1], rz_rs.at[d - 1], me, z ^ d)
+
+    for d in range(1, n_ha):
+        share_rz(d).start()
+    for d in range(1, n_ha):
+        share_rz(d).wait()
+    dots = rz[z]
+    for d in range(1, n_ha):
+        dots = dots + rz_in[d - 1]
+    dot = jnp.sum(dots, axis=1, keepdims=True)[0:r]
+    inv = inv_own[z][:, 0:1]
+    back = inv * inv * dot / D
+
+    for d in range(1, n_ha):
+        finish(d).wait()
+    own_rows = own[z]
+    acc[0:r, :] = own_rows
+    for d in range(1, n_ha):
+        tail[...] = fr[d - 1].astype(F32)
+        for q in range(4):
+            acc[0:r, q * cols4:(q + 1) * cols4] += tail[q * r:(q + 1) * r, :]
+    scaled = acc[0:r, :] * gain[...]
+    out[...] = (go[...].astype(F32) + inv * scaled - res[...].astype(F32) * back).astype(BF16)
+
+
+def fused_call(n_wa, n_ha, residual_in, grad_out, norm_gain, w_gate, w_up, w_down):
+    r, width = residual_in.shape
+    rows, half, n_chip = r * n_ha, r * n_ha // 2, n_wa // 2
+    ch = w_gate.shape[1] // CHUNKS
+    sub = ch // n_chip
+    vmem, dma = pltpu.VMEM, pltpu.SemaphoreType.DMA
+    inside, outside = pl.BlockSpec(memory_space=pltpu.VMEM), pl.BlockSpec(memory_space=pl.ANY)
+    return pl.pallas_call(
+        functools.partial(fused, n_wa, n_ha),
+        out_shape=jax.ShapeDtypeStruct((r, width), BF16),
+        in_specs=[inside] * 3 + [outside] * 3,
+        out_specs=inside,
+        scratch_shapes=[
+            vmem((DEEP, width, ch), BF16), vmem((DEEP, width, ch), BF16), vmem((DEEP_DOWN, ch, width), BF16),
+            vmem((n_ha, 4 * r, width // 2), BF16), vmem((4 * r, width // 2), F32),
+            vmem((rows, width), F32), vmem((rows, width), F32),
+            vmem((rows, width), BF16), vmem((rows, width), BF16),
+            vmem((rows, 128), F32), vmem((n_wa - 1, rows, 128), F32),
+            vmem((2, half, 128), F32), vmem((n_ha, r, 128), F32),
+            vmem((SLOTS, 2, 3 * half, ch), F32), vmem((SLOTS, 3 * half, ch), F32),
+            vmem((SLOTS, n_chip, 3 * half, sub), F32), vmem((SLOTS, n_chip - 1, 3 * half, sub), F32),
+            vmem((CHUNKS, 2, n_chip, 2 * half, sub), BF16),
+            vmem((rows, width), F32),
+            vmem((half, 128), F32), vmem((n_wa - 1, half, 128), F32),
+            vmem((n_ha, 16, 128), F32), vmem((n_ha - 1, 16, 128), F32),
+            vmem((n_ha, r, width), F32),
+            vmem((n_ha, 4 * r, width // 4), BF16), vmem((n_ha - 1, 4 * r, width // 4), BF16),
+            vmem((4 * r, width // 4), F32),
+            dma((DEEP,)), dma((DEEP,)), dma((DEEP_DOWN,)),
+            dma((n_ha - 1,)), dma((n_ha - 1,)),
+            dma((n_wa - 1,)), dma((n_wa - 1,)),
+            dma((SLOTS,)), dma((SLOTS,)),
+            dma((SLOTS, n_chip - 1)), dma((SLOTS, n_chip - 1)),
+            dma((SLOTS, n_chip - 1)), dma((SLOTS, n_chip - 1)),
+            dma((SLOTS,)), dma((SLOTS,)),
+            dma((n_wa - 1,)), dma((n_wa - 1,)),
+            dma((n_ha - 1,)), dma((n_ha - 1,)),
+            dma((n_ha - 1,)), dma((n_ha - 1,)),
+        ],
+        compiler_params=pltpu.CompilerParams(
+            collective_id=0, has_side_effects=True, vmem_limit_bytes=63 * 1024 * 1024
+        ),
+    )(residual_in, grad_out, norm_gain.astype(F32).reshape(1, width), w_gate, w_up, w_down)
 
 
 def gate_grads(gate, up, d_hidden):
@@ -47,8 +364,25 @@
     return grad_in.astype(jnp.bfloat16)
 
 
+def fits(mesh, residual_in, w_gate):
+    n_wa, n_ha = mesh.shape["wa"], mesh.shape["ha"]
+    r, hidden = residual_in.shape[0], w_gate.shape[1]
+    powers = all(n >= 2 and n & (n - 1) == 0 for n in (n_wa, n_ha)) and n_wa >= 4
+    return (
+        powers
+        and hidden % (CHUNKS * 128 * (n_wa // 2)) == 0
+        and (r * n_ha) % 16 == 0
+        and r % 4 == 0
+        and r <= 16
+    )
+
+
 def solution(mesh):
     placed = (P("ha", "wa"), P("ha", "wa"), P("wa"), P("wa", "ha"), P("wa", "ha"), P("ha", "wa"))
-    return jax.shard_map(
-        local, mesh=mesh, in_specs=placed, out_specs=P("ha", "wa"), check_vma=False
-    )
+
+    def part(*args):
+        if fits(mesh, args[0], args[3]):
+            return fused_call(mesh.shape["wa"], mesh.shape["ha"], *args)
+        return local(*args)
+
+    return jax.shard_map(part, mesh=mesh, in_specs=placed, out_specs=P("ha", "wa"), check_vma=False)

time: 229 us -> 80.7 us (0.35)
  Pallas kernels: 0 us -> 77.7 us
  waiting for transfers between devices: 77.7 us -> 0 us
  matrix products: 64.8 us -> 0 us
  blocking collectives: 60.6 us -> 0 us
  between operations: 14.2 us -> 0.01 us
  other arithmetic: 7.73 us -> 1.29 us
    pallas_call x0 -> x1, Pallas kernels: none -> 77.7 us  [fused_call(): pl.pallas_call(functools.partial(fused, n_wa, n_ha), out_shape=jax.ShapeD...]
    psum x1 -> x0, waiting for transfers between devices: 76.4 us -> none  [local(): summed = lax.psum(partial_sums, 'wa')]
    dot_general x5 -> x0, matrix products: 64.8 us -> none  [the longest x1 14.4 us: local(): lax.dot_general(piece[1], w_down, (((1,), (1,)), ((), ())), preferred_ele...]
    psum x2 -> x0, blocking collectives: 26.9 us -> none  [the longest x1 15.1 us: local(): squares = lax.psum(jnp.sum(stream * stream, axis=1), 'wa')]
    unnamed x1 -> x0, blocking collectives: 18.6 us -> none
    all_gather x1 -> x0, blocking collectives: 15.1 us -> none  [local(): piece = lax.all_gather(stacked, 'ha', axis=1, tiled=True)]
    another operation x3 -> x0, other arithmetic: 5.18 us -> none  [the longest x1 3.39 us: local(): partial_sums = jnp.stack([gate_part, up_part, back_part])]
  transfers between devices with their start and end apart: 2 -> 0, of which waited for: 2 -> 0; matrix products, arithmetic and copies ran while one was open for 0% -> 0% of each run, Pallas kernels for 0% -> 0%
where the time goes in v1:
time: 80.7 us; the launch traced here: 80.4 us
  Pallas kernels  77.7 us (96%)
  local copies, waits for them, and re-layouts  1.47 us (2%)
  other arithmetic  1.29 us (2%)
    pallas_call x1, Pallas kernels, fused_call(): pl.pallas_call(functools.partial(fused, n_wa, n_ha), out_shape=jax.ShapeD...  77.7 us

profile of v1, /device:TPU:0, one launch (start us, length us, event | category | flops | bytes accessed | tf_op | source)
XLA Modules:
  0.0 80.4 jit_solution(15218309316673786007)
XLA Ops:
  0.0 1.3 %reshape.7 = f32[2048]{0:T(1024)} convert(bf16[2048]{0:T(1024)(128)(2,1)} %param.8) | non-fusion elementwise | flops 2048 | bytes 12288 | tf_op jit(solution)/shard_map/reshape | solution.py:323
  1.3 77.7 %shard_map.64 = bf16[12,2048]{1,0:T(8,128)(2,1)} custom-call(bf16[12,2048]{1,0:T(8,128)(2,1)} %res.1, bf16[12,2048]{1,0:T(8,128)(2,1)} %go.1, f32[1,2048]{1,0:T(1,128)} %bitcast.1, bf16[2048,6656]{1,0:T(8,128)(2,1)} %wg.1, bf16[2048,6656]{1,0:T(8,128)(2,1)} %wu.1, bf16[6656,2048]{1,0:T(8,128)(2,1)} %wd.1), custom_call_target="tpu_custom_call" | custom-call | tf_op jit(solution)/shard_map/pallas_call | solution.py:288
  79.0 1.5 %copy.8 = bf16[12,2048]{1,0:T(8,128)(2,1)} copy(bf16[12,2048]{1,0:T(8,128)(2,1)} %shard_map.64) | data formatting | bytes 98304
